TPU v7x, 256 devices: a whole 4x4x8 slice. The times are simulated.
256 devices in a mesh: gx: 4 (over z_hi), gy: 4 (over z_lo, core), gz: 16 (over y, x).
Axes of the slice: x: 4, y: 4, z: 8 (z_hi: 4, z_lo: 2; z = z_hi * 2 + z_lo), core: 2. Of those that a mesh axis runs over, the one named last changes fastest.
Arguments:
- near_modes: float32 [4, 4, 64, 24, 512], P('gx', 'gy', 'gz'), may hold values from -0.375 to 0.375
- diag_blocks: float32 [4, 4, 64, 512, 512], P('gx', 'gy', 'gz'), may hold values from -1 to 4
- face_blocks: float32 [4, 4, 64, 6, 128, 512], P('gx', 'gy', 'gz'), may hold values from -0.5 to 0.5
- face_rows: int32 [4, 4, 64, 6, 128], P('gx', 'gy', 'gz'), may hold values from 0 to 511, as said below
- coarse_modes: float32 [4, 4, 64, 24, 24], P('gx', 'gy', 'gz'), may hold values from -0.15625 to 0.15625
Outputs:
- coarse1: float32 [4, 4, 64, 24, 168], P('gx', 'gy', 'gz')
- coarse2: float32 [4, 4, 24, 120], P('gx', 'gy')
Inputs may be any that keep to these rules, and one draw needn't show every extreme that they name: `face_rows`: for every aggregate and face the 128 row numbers are distinct.
All inputs are finite; a program needn't handle non-finite values.
Results may differ from a plain program's by a relative error of at most 0.000057.
Values sent between devices are 32-bit elements; how exact they have to be, the bound alone decides.
A program may use at most 320 MiB of HBM per device.

v0:
```python
import jax
import jax.numpy as jnp
from jax import lax
from jax.sharding import PartitionSpec as P

HIGHEST = lax.Precision.HIGHEST
OMEGA_FINE = 2.0 / 3.0
OMEGA_COARSE = 1.0
EPSILON = 1e-06


def padded_2(block, sides, width):
    for axis, dim in sides:
        count = lax.axis_size(axis)
        forward = [(i, i + 1) for i in range(count - 1)]
        backward = [(target, source) for source, target in forward]
        low = lax.ppermute(
            lax.slice_in_dim(block, block.shape[dim] - width, None, axis=dim), axis, forward
        )
        high = lax.ppermute(lax.slice_in_dim(block, 0, width, axis=dim), axis, backward)
        block = jnp.concatenate([low, block, high], axis=dim)
    return block


def neighbours(padded):
    return jnp.stack(
        [
            padded[:-2, 1:-1, 1:-1],
            padded[2:, 1:-1, 1:-1],
            padded[1:-1, :-2, 1:-1],
            padded[1:-1, 2:, 1:-1],
            padded[1:-1, 1:-1, :-2],
            padded[1:-1, 1:-1, 2:],
        ],
        axis=3,
    )


def make_selector(face_rows, dof_count):
    columns = lax.broadcasted_iota(jnp.int32, face_rows.shape + (dof_count,), 3)
    return (face_rows[..., None] == columns).astype(jnp.float32)


def smooth_fine(modes, near, diag_blocks, face_blocks, selector):
    product = jnp.einsum("nkc,nrc->nkr", modes, diag_blocks, precision=HIGHEST)
    face_terms = jnp.einsum("nfkc,nfhc->nfkh", near, face_blocks, precision=HIGHEST)
    product = product + jnp.einsum("nfkh,nfhr->nkr", face_terms, selector, precision=HIGHEST)
    diagonal = jnp.diagonal(diag_blocks, axis1=1, axis2=2)
    return modes - OMEGA_FINE * product / diagonal[:, None, :]


def galerkin_fine(smoothed, near_smoothed, diag_blocks, face_blocks, selector):
    applied = jnp.einsum("nkc,nrc->nkr", smoothed, diag_blocks, precision=HIGHEST)
    own_block = jnp.einsum("nir,njr->nij", smoothed, applied, precision=HIGHEST)
    picked = jnp.einsum("nir,nfhr->nifh", smoothed, selector, precision=HIGHEST)
    across = jnp.einsum("nfkc,nfhc->nfkh", near_smoothed, face_blocks, precision=HIGHEST)
    lateral = jnp.einsum("nifh,nfjh->nfij", picked, across, precision=HIGHEST)
    blocks = jnp.concatenate([own_block[:, None], lateral], axis=1)
    agg_count, modes_count = (own_block.shape[0], own_block.shape[1])
    return jnp.transpose(blocks, (0, 2, 1, 3)).reshape(agg_count, modes_count, 7 * modes_count)


def split_rows(coarse):
    agg_count, modes_count = (coarse.shape[0], coarse.shape[1])
    blocks = jnp.transpose(coarse.reshape(agg_count, modes_count, 7, modes_count), (0, 2, 1, 3))
    return (blocks[:, 0], blocks[:, 1:])


def smooth_coarse(coarse, modes, near_modes):
    own_block, lateral = split_rows(coarse)
    row_scale = jnp.sum(jnp.abs(coarse), axis=2) + EPSILON
    product = jnp.einsum("nij,njk->nik", own_block, modes, precision=HIGHEST)
    product = product + jnp.einsum("nfij,nfjk->nik", lateral, near_modes, precision=HIGHEST)
    return modes - OMEGA_COARSE * product / row_scale[:, :, None]


def galerkin_partials(coarse, smoothed, near_smoothed):
    own_block, lateral = split_rows(coarse)
    applied = jnp.einsum("nij,njl->nil", own_block, smoothed, precision=HIGHEST)
    centre = jnp.einsum("nik,nil->nkl", smoothed, applied, precision=HIGHEST)
    reached = jnp.einsum("nfij,nfjl->nfil", lateral, near_smoothed, precision=HIGHEST)
    face_terms = jnp.einsum("nik,nfil->nfkl", smoothed, reached, precision=HIGHEST)
    centre = centre + face_terms[:, 4] + face_terms[:, 5]
    return jnp.stack(
        [centre, face_terms[:, 0], face_terms[:, 1], face_terms[:, 2], face_terms[:, 3]], axis=1
    )


def per_device(near_modes, diag_blocks, face_blocks, face_rows, coarse_modes):
    grid_shape = near_modes.shape[:3]
    dof_count = near_modes.shape[4]

    def flatten(array_in):
        return array_in.reshape(
            (array_in.shape[0] * array_in.shape[1] * array_in.shape[2],) + array_in.shape[3:]
        )

    def ungrid(array_in):
        return array_in.reshape(grid_shape + array_in.shape[1:])

    selector = make_selector(flatten(face_rows), dof_count)
    padded = padded_2(near_modes, (("gx", 0), ("gy", 1), ("gz", 2)), 1)
    padded_coarse = padded_2(coarse_modes, (("gx", 0), ("gy", 1), ("gz", 2)), 1)
    smoothed = smooth_fine(
        flatten(near_modes),
        flatten(neighbours(padded)),
        flatten(diag_blocks),
        flatten(face_blocks),
        selector,
    )
    padded_smoothed = padded_2(ungrid(smoothed), (("gx", 0), ("gy", 1), ("gz", 2)), 1)
    coarse_one = galerkin_fine(
        smoothed,
        flatten(neighbours(padded_smoothed)),
        flatten(diag_blocks),
        flatten(face_blocks),
        selector,
    )
    coarse_smoothed = smooth_coarse(
        coarse_one, flatten(coarse_modes), flatten(neighbours(padded_coarse))
    )
    padded_result = padded_2(ungrid(coarse_smoothed), (("gx", 0), ("gy", 1), ("gz", 2)), 1)
    near_result = flatten(neighbours(padded_result))
    partials = galerkin_partials(coarse_one, coarse_smoothed, near_result)
    column = lax.psum(jnp.sum(partials, axis=0), "gz")
    modes_count = coarse_modes.shape[3]
    coarse_two = jnp.transpose(column, (1, 0, 2)).reshape(1, 1, modes_count, 5 * modes_count)
    return (ungrid(coarse_one), coarse_two)


def solution(mesh):
    placed = (
        P("gx", "gy", "gz", None, None),
        P("gx", "gy", "gz", None, None),
        P("gx", "gy", "gz", None, None, None),
        P("gx", "gy", "gz", None, None),
        P("gx", "gy", "gz", None, None),
    )
    return jax.shard_map(
        per_device,
        mesh=mesh,
        in_specs=placed,
        out_specs=(P("gx", "gy", "gz", None, None), P("gx", "gy", None, None)),
        check_vma=False,
    )
```

profile of v0, /device:TPU:32, one launch (start us, length us, event | category | flops | bytes accessed | tf_op | source)
XLA Modules:
  0.0 298.9 jit_solution(7215421535686690841)
XLA Ops:
  0.6 5.2 %collective-permute-start = (f32[1,1,4,24,512]{4,3,2,1,0:T(8,128)}, f32[1,1,4,24,512]{4,3,2,1,0:T(8,128)S(1)}, u32[]{:S(2)}, u32[]{:S(2)}) collective-permute-start(f32[1,1,4,24,512]{4,3,2,1,0:T(8,128)} %param.5), channel_id=1, source_target_pairs={{0,64},{64,128},{128,192},{1,65},{65,129},{129,193},{2,66},{66,130... | collective-permute-start | bytes 589832 | tf_op jit(solution)/shard_map/ppermute | solution.py:17
  5.8 1.3 collective-permute-start.1
  7.1 6.1 %collective-permute-start.12 = (f32[1,1,4,24,24]{4,3,2,1,0:T(8,128)}, f32[1,1,4,24,24]{4,3,2,1,0:T(8,128)S(1)}, u32[]{:S(2)}, u32[]{:S(2)}) collective-permute-start(f32[1,1,4,24,24]{4,3,2,1,0:T(8,128)} %param.9), channel_id=1, source_target_pairs={{0,64},{64,128},{128,192},{1,65},{65,129},{129,193},{2,66},{66,130... | collective-permute-start | bytes 27656 | tf_op jit(solution)/shard_map/ppermute | solution.py:17
  13.2 1.3 collective-permute-start.13
  15.3 61.7 %copy.37 = f32[1,1,4,512,512]{2,4,3,1,0:T(8,128)} copy(f32[1,1,4,512,512]{4,3,2,1,0:T(8,128)} %param.6) | data formatting | bytes 8388608 | tf_op args[1]
  77.0 5.5 %gather_fusion = f32[512,4]{1,0:T(8,128)S(1)} fusion(f32[4,512,512]{0,2,1:T(8,128)} %bitcast.1, s32[512]{0:T(512)S(1)} %bitcast.194), kind=kCustom, calls=%fused_computation | custom fusion | bytes 20480 | tf_op jit(solution)/shard_map/jit(diagonal)/gather | solution.py:48
  82.7 1.9 collective-permute-start.14
  84.6 3.6 %collective-permute-start.15 = (f32[3,1,4,24,24]{4,3,2,1,0:T(8,128)S(1)}, f32[3,1,4,24,24]{4,3,2,1,0:T(8,128)S(1)}, u32[]{:S(2)}, u32[]{:S(2)}) collective-permute-start(f32[3,1,4,24,24]{4,3,2,1,0:T(8,128)S(1)} %constant_dynamic-update-slice_fusion.3), channel_id=1, source_target_pairs={{16,0},{32,16},{48,32},{17,1},{33,17},{49,33},{18,2},{34,18},{50,3... | collective-permute-start | bytes 82952 | tf_op jit(solution)/shard_map/ppermute | solution.py:20
  89.2 1.8 collective-permute-done.15
  91.0 3.7 %collective-permute-start.16 = (f32[3,3,1,24,24]{4,3,2,1,0:T(8,128)S(1)}, f32[3,3,1,24,24]{4,3,2,1,0:T(8,128)S(1)}, u32[]{:S(2)}, u32[]{:S(2)}) collective-permute-start(f32[3,3,1,24,24]{4,3,2,1,0:T(8,128)S(1)} %get-tuple-element.15), channel_id=1, source_target_pairs={{0,1},{1,2},{2,3},{3,4},{4,5},{5,6},{6,7},{7,8},{8,9},{9,10},{10,1... | collective-permute-start | bytes 62216 | tf_op jit(solution)/shard_map/ppermute | solution.py:17
  94.6 1.3 collective-permute-start.17
  96.1 1.9 collective-permute-start.2
  98.0 3.6 %collective-permute-start.3 = (f32[3,1,4,24,512]{4,3,2,1,0:T(8,128)S(1)}, f32[3,1,4,24,512]{4,3,2,1,0:T(8,128)S(1)}, u32[]{:S(2)}, u32[]{:S(2)}) collective-permute-start(f32[3,1,4,24,512]{4,3,2,1,0:T(8,128)S(1)} %constant_dynamic-update-slice_fusion), channel_id=1, source_target_pairs={{16,0},{32,16},{48,32},{17,1},{33,17},{49,33},{18,2},{34,18},{50,3... | collective-permute-start | bytes 1769480 | tf_op jit(solution)/shard_map/ppermute | solution.py:20
  101.7 5.5 %collective-permute-done.2 = f32[3,1,4,24,512]{4,3,2,1,0:T(8,128)S(1)} collective-permute-done((f32[3,1,4,24,512]{4,3,2,1,0:T(8,128)S(1)}, f32[3,1,4,24,512]{4,3,2,1,0:T(8,128)S(1)}, u32[]{:S(2)}, u32[]{:S(2)}) %collective-permute-start.2) | collective-permute-done | bytes 589856 | tf_op jit(solution)/shard_map/ppermute | solution.py:17
  107.3 1.8 collective-permute-done.3
  109.1 4.6 %collective-permute-start.4 = (f32[3,3,1,24,512]{4,3,2,1,0:T(8,128)S(1)}, f32[3,3,1,24,512]{4,3,2,1,0:T(8,128)S(1)}, u32[]{:S(2)}, u32[]{:S(2)}) collective-permute-start(f32[3,3,1,24,512]{4,3,2,1,0:T(8,128)S(1)} %get-tuple-element.11), channel_id=1, source_target_pairs={{0,1},{1,2},{2,3},{3,4},{4,5},{5,6},{6,7},{7,8},{8,9},{9,10},{10,1... | collective-permute-start | bytes 1327112 | tf_op jit(solution)/shard_map/ppermute | solution.py:17
  113.7 1.5 collective-permute-start.5
  115.2 4.2 %collective-permute-done.4 = f32[3,3,1,24,512]{4,3,2,1,0:T(8,128)S(1)} collective-permute-done((f32[3,3,1,24,512]{4,3,2,1,0:T(8,128)S(1)}, f32[3,3,1,24,512]{4,3,2,1,0:T(8,128)S(1)}, u32[]{:S(2)}, u32[]{:S(2)}) %collective-permute-start.4) | collective-permute-done | bytes 442400 | tf_op jit(solution)/shard_map/ppermute | solution.py:17
  119.5 4.4 %collective-permute-done.5 = f32[3,3,1,24,512]{4,3,2,1,0:T(8,128)S(1)} collective-permute-done((f32[3,3,1,24,512]{4,3,2,1,0:T(8,128)S(1)}, f32[3,3,1,24,512]{4,3,2,1,0:T(8,128)S(1)}, u32[]{:S(2)}, u32[]{:S(2)}) %collective-permute-start.5) | collective-permute-done | bytes 442400 | tf_op jit(solution)/shard_map/ppermute | solution.py:20
  123.9 5.4 %fusion.2 = f32[4,6,24,128]{3,2,1,0:T(8,128)S(1)} fusion(f32[1,1,4,6,128,512]{5,4,3,2,1,0:T(8,128)S(1)} %bitcast.196, f32[1,1,4,6,24,512]{5,4,3,2,1,0:T(8,128)S(1)} %fusion.43), kind=kOutput, calls=%fused_computation.3 | convolution fusion | flops 452984832 | bytes 7766016 | tf_op jit(solution)/shard_map/nfkc,nfhc->nfkh/dot_general | solution.py:46
  129.3 2.3 fusion.26
  131.6 3.6 %fusion.23 = f32[4,24,512]{2,1,0:T(8,128)S(1)} fusion(f32[4,24,512]{2,1,0:T(8,128)S(1)} %fusion.26, f32[1,1,4,512,512]{4,3,2,1,0:T(8,128)S(1)} %copy-done, f32[1,1,4,24,512]{4,3,2,1,0:T(8,128)S(1)} %copy-done.1, f32[4,512]{1,0:T(4,128)S(1)} %copy.45), kind=kOutput, calls=%fused_computation.20 | convolution fusion | flops 302186496 | bytes 4792320 | tf_op jit(solution)/shard_map/nkc,nrc->nkr/dot_general | solution.py:45
  135.2 3.6 %fusion.8 = f32[4,24,512]{2,1,0:T(8,128)S(1)} fusion(f32[4,24,512]{2,1,0:T(8,128)S(1)} %fusion.23, f32[1,1,4,512,512]{4,3,2,1,0:T(8,128)S(1)} %copy-done), kind=kOutput, calls=%fused_computation.10 | convolution fusion | flops 301989888 | bytes 4587520 | tf_op jit(solution)/shard_map/nkc,nrc->nkr/dot_general | solution.py:53
  138.7 6.7 %collective-permute-start.6 = (f32[1,1,4,24,512]{4,3,2,1,0:T(8,128)S(1)}, f32[1,1,4,24,512]{4,3,2,1,0:T(8,128)S(1)}, u32[]{:S(2)}, u32[]{:S(2)}) collective-permute-start(f32[1,1,4,24,512]{4,3,2,1,0:T(8,128)S(1)} %bitcast.197), channel_id=1, source_target_pairs={{0,64},{64,128},{128,192},{1,65},{65,129},{129,193},{2,66},{66,130... | collective-permute-start | bytes 589832 | tf_op jit(solution)/shard_map/ppermute | solution.py:17
  145.4 1.5 collective-permute-start.7
  146.9 3.1 %fusion.4 = f32[4,24,6,128]{3,1,2,0:T(8,128)S(1)} fusion(s32[4,6,128]{2,1,0:T(8,128)S(1)} %copy.44, f32[4,24,512]{2,1,0:T(8,128)S(1)} %fusion.23), kind=kOutput, calls=%fused_computation.6 | convolution fusion | flops 454557696 | bytes 503808 | tf_op jit(solution)/shard_map/nir,nfhr->nifh/dot_general | solution.py:55
  150.4 6.4 %collective-permute-done.7 = f32[1,1,4,24,512]{4,3,2,1,0:T(8,128)S(1)} collective-permute-done((f32[1,1,4,24,512]{4,3,2,1,0:T(8,128)S(1)}, f32[1,1,4,24,512]{4,3,2,1,0:T(8,128)S(1)}, u32[]{:S(2)}, u32[]{:S(2)}) %collective-permute-start.7) | collective-permute-done | bytes 196640 | tf_op jit(solution)/shard_map/ppermute | solution.py:20
  156.8 1.9 collective-permute-start.8
  158.7 3.6 %collective-permute-start.9 = (f32[3,1,4,24,512]{4,3,2,1,0:T(8,128)S(1)}, f32[3,1,4,24,512]{4,3,2,1,0:T(8,128)S(1)}, u32[]{:S(2)}, u32[]{:S(2)}) collective-permute-start(f32[3,1,4,24,512]{4,3,2,1,0:T(8,128)S(1)} %pad_maximum_fusion), channel_id=1, source_target_pairs={{16,0},{32,16},{48,32},{17,1},{33,17},{49,33},{18,2},{34,18},{50,3... | collective-permute-start | bytes 1769480 | tf_op jit(solution)/shard_map/ppermute | solution.py:20
  162.8 5.3 %collective-permute-done.8 = f32[3,1,4,24,512]{4,3,2,1,0:T(8,128)S(1)} collective-permute-done((f32[3,1,4,24,512]{4,3,2,1,0:T(8,128)S(1)}, f32[3,1,4,24,512]{4,3,2,1,0:T(8,128)S(1)}, u32[]{:S(2)}, u32[]{:S(2)}) %collective-permute-start.8) | collective-permute-done | bytes 589856 | tf_op jit(solution)/shard_map/ppermute | solution.py:17
  168.0 1.8 collective-permute-done.9
  169.9 3.4 %collective-permute-start.10 = (f32[3,3,1,24,512]{4,3,2,1,0:T(8,128)S(1)}, f32[3,3,1,24,512]{4,3,2,1,0:T(8,128)S(1)}, u32[]{:S(2)}, u32[]{:S(2)}) collective-permute-start(f32[3,3,1,24,512]{4,3,2,1,0:T(8,128)S(1)} %get-tuple-element.9), channel_id=1, source_target_pairs={{0,1},{1,2},{2,3},{3,4},{4,5},{5,6},{6,7},{7,8},{8,9},{9,10},{10,1... | collective-permute-start | bytes 1327112 | tf_op jit(solution)/shard_map/ppermute | solution.py:17
  173.3 1.3 collective-permute-start.11
  174.6 4.4 %collective-permute-done.10 = f32[3,3,1,24,512]{4,3,2,1,0:T(8,128)S(1)} collective-permute-done((f32[3,3,1,24,512]{4,3,2,1,0:T(8,128)S(1)}, f32[3,3,1,24,512]{4,3,2,1,0:T(8,128)S(1)}, u32[]{:S(2)}, u32[]{:S(2)}) %collective-permute-start.10) | collective-permute-done | bytes 442400 | tf_op jit(solution)/shard_map/ppermute | solution.py:17
  179.1 4.4 %collective-permute-done.11 = f32[3,3,1,24,512]{4,3,2,1,0:T(8,128)S(1)} collective-permute-done((f32[3,3,1,24,512]{4,3,2,1,0:T(8,128)S(1)}, f32[3,3,1,24,512]{4,3,2,1,0:T(8,128)S(1)}, u32[]{:S(2)}, u32[]{:S(2)}) %collective-permute-start.11) | collective-permute-done | bytes 442400 | tf_op jit(solution)/shard_map/ppermute | solution.py:20
  183.5 5.4 %fusion = f32[4,6,24,128]{3,2,1,0:T(8,128)S(1)} fusion(f32[1,1,4,6,128,512]{5,4,3,2,1,0:T(8,128)S(1)} %bitcast.196, f32[1,1,4,6,24,512]{5,4,2,3,1,0:T(8,128)S(1)} %fusion.37), kind=kOutput, calls=%fused_computation.1 | convolution fusion | flops 452984832 | bytes 7766016 | tf_op jit(solution)/shard_map/nfkc,nfhc->nfkh/dot_general | solution.py:56
  190.8 6.1 %collective-permute-start.18 = (f32[1,1,4,24,24]{4,3,2,1,0:T(8,128)S(1)}, f32[1,1,4,24,24]{4,3,2,1,0:T(8,128)S(1)}, u32[]{:S(2)}, u32[]{:S(2)}) collective-permute-start(f32[1,1,4,24,24]{4,3,2,1,0:T(8,128)S(1)} %bitcast.203), channel_id=1, source_target_pairs={{0,64},{64,128},{128,192},{1,65},{65,129},{129,193},{2,66},{66,130... | collective-permute-start | bytes 27656 | tf_op jit(solution)/shard_map/ppermute | solution.py:17
  196.9 1.3 collective-permute-start.19
  199.1 4.9 %collective-permute-done.19 = f32[1,1,4,24,24]{4,3,2,1,0:T(8,128)S(1)} collective-permute-done((f32[1,1,4,24,24]{4,3,2,1,0:T(8,128)S(1)}, f32[1,1,4,24,24]{4,3,2,1,0:T(8,128)S(1)}, u32[]{:S(2)}, u32[]{:S(2)}) %collective-permute-start.19) | collective-permute-done | bytes 9248 | tf_op jit(solution)/shard_map/ppermute | solution.py:20
  204.0 1.9 collective-permute-start.20
  205.9 3.6 %collective-permute-start.21 = (f32[3,1,4,24,24]{4,3,2,1,0:T(8,128)S(1)}, f32[3,1,4,24,24]{4,3,2,1,0:T(8,128)S(1)}, u32[]{:S(2)}, u32[]{:S(2)}) collective-permute-start(f32[3,1,4,24,24]{4,3,2,1,0:T(8,128)S(1)} %pad_maximum_fusion.26), channel_id=1, source_target_pairs={{16,0},{32,16},{48,32},{17,1},{33,17},{49,33},{18,2},{34,18},{50,3... | collective-permute-start | bytes 82952 | tf_op jit(solution)/shard_map/ppermute | solution.py:20
  210.5 1.8 collective-permute-done.21
  212.3 5.8 %collective-permute-start.22 = (f32[3,3,1,24,24]{4,3,2,1,0:T(8,128)S(1)}, f32[3,3,1,24,24]{4,3,2,1,0:T(8,128)S(1)}, u32[]{:S(2)}, u32[]{:S(2)}) collective-permute-start(f32[3,3,1,24,24]{4,3,2,1,0:T(8,128)S(1)} %get-tuple-element.13), channel_id=1, source_target_pairs={{0,1},{1,2},{2,3},{3,4},{4,5},{5,6},{6,7},{7,8},{8,9},{9,10},{10,1... | collective-permute-start | bytes 62216 | tf_op jit(solution)/shard_map/ppermute | solution.py:17
  218.0 1.3 collective-permute-start.23
  219.4 1.0 collective-permute-done.22
  220.3 4.3 %collective-permute-done.23 = f32[3,3,1,24,24]{4,3,2,1,0:T(8,128)S(1)} collective-permute-done((f32[3,3,1,24,24]{4,3,2,1,0:T(8,128)S(1)}, f32[3,3,1,24,24]{4,3,2,1,0:T(8,128)S(1)}, u32[]{:S(2)}, u32[]{:S(2)}) %collective-permute-start.23) | collective-permute-done | bytes 20768 | tf_op jit(solution)/shard_map/ppermute | solution.py:20
  225.4 1.6 convolution_bitcast_fusion
  227.4 71.5 %psum.7 = f32[1,1,24,120]{3,2,1,0:T(8,128)} all-reduce(f32[1,1,24,120]{3,2,1,0:T(8,128)S(1)} %reshape.55), channel_id=1, replica_groups=mesh['gx'=4,'gy'=4,'gz'=16] {'gz'}, use_global_device_ids=true, to_apply=%region_2.3 | all-reduce | flops 2880 | bytes 23040 | tf_op jit(solution)/shard_map/psum | solution.py:125
  (75 shorter events, 7.6 us)
Async XLA Ops:
  0.6 95.3 %collective-permute-start = (f32[1,1,4,24,512]{4,3,2,1,0:T(8,128)}, f32[1,1,4,24,512]{4,3,2,1,0:T(8,128)S(1)}, u32[]{:S(2)}, u32[]{:S(2)}) collective-permute-start(f32[1,1,4,24,512]{4,3,2,1,0:T(8,128)} %param.5), channel_id=1, source_target_pairs={{0,64},{64,128},{128,192},{1,65},{65,129},{129,193},{2,66},{66,130... | collective-permute-start | bytes 589832 | tf_op jit(solution)/shard_map/ppermute | solution.py:17
  5.8 90.2 %collective-permute-start.1 = (f32[1,1,4,24,512]{4,3,2,1,0:T(8,128)}, f32[1,1,4,24,512]{4,3,2,1,0:T(8,128)S(1)}, u32[]{:S(2)}, u32[]{:S(2)}) collective-permute-start(f32[1,1,4,24,512]{4,3,2,1,0:T(8,128)} %param.5), channel_id=1, source_target_pairs={{64,0},{128,64},{192,128},{65,1},{129,65},{193,129},{66,2},{130,66... | collective-permute-start | bytes 589832 | tf_op jit(solution)/shard_map/ppermute | solution.py:20
  7.1 75.5 %collective-permute-start.12 = (f32[1,1,4,24,24]{4,3,2,1,0:T(8,128)}, f32[1,1,4,24,24]{4,3,2,1,0:T(8,128)S(1)}, u32[]{:S(2)}, u32[]{:S(2)}) collective-permute-start(f32[1,1,4,24,24]{4,3,2,1,0:T(8,128)} %param.9), channel_id=1, source_target_pairs={{0,64},{64,128},{128,192},{1,65},{65,129},{129,193},{2,66},{66,130... | collective-permute-start | bytes 27656 | tf_op jit(solution)/shard_map/ppermute | solution.py:17
  13.2 69.4 %collective-permute-start.13 = (f32[1,1,4,24,24]{4,3,2,1,0:T(8,128)}, f32[1,1,4,24,24]{4,3,2,1,0:T(8,128)S(1)}, u32[]{:S(2)}, u32[]{:S(2)}) collective-permute-start(f32[1,1,4,24,24]{4,3,2,1,0:T(8,128)} %param.9), channel_id=1, source_target_pairs={{64,0},{128,64},{192,128},{65,1},{129,65},{193,129},{66,2},{130,66... | collective-permute-start | bytes 27656 | tf_op jit(solution)/shard_map/ppermute | solution.py:20
  15.3 67.4 %copy-start.2 = (f32[1,1,4,24,24]{4,3,2,1,0:T(8,128)S(1)}, f32[1,1,4,24,24]{4,3,2,1,0:T(8,128)}, u32[]{:S(2)}) copy-start(f32[1,1,4,24,24]{4,3,2,1,0:T(8,128)} %param.9) | copy-start | bytes 27652
  77.0 19.0 %copy-start.1 = (f32[1,1,4,24,512]{4,3,2,1,0:T(8,128)S(1)}, f32[1,1,4,24,512]{4,3,2,1,0:T(8,128)}, u32[]{:S(2)}) copy-start(f32[1,1,4,24,512]{4,3,2,1,0:T(8,128)} %param.5) | copy-start | bytes 589828
  82.7 6.5 %collective-permute-start.14 = (f32[3,1,4,24,24]{4,3,2,1,0:T(8,128)S(1)}, f32[3,1,4,24,24]{4,3,2,1,0:T(8,128)S(1)}, u32[]{:S(2)}, u32[]{:S(2)}) collective-permute-start(f32[3,1,4,24,24]{4,3,2,1,0:T(8,128)S(1)} %constant_dynamic-update-slice_fusion.3), channel_id=1, source_target_pairs={{0,16},{16,32},{32,48},{1,17},{17,33},{33,49},{2,18},{18,34},{34,5... | collective-permute-start | bytes 82952 | tf_op jit(solution)/shard_map/ppermute | solution.py:17
  84.6 6.3 %collective-permute-start.15 = (f32[3,1,4,24,24]{4,3,2,1,0:T(8,128)S(1)}, f32[3,1,4,24,24]{4,3,2,1,0:T(8,128)S(1)}, u32[]{:S(2)}, u32[]{:S(2)}) collective-permute-start(f32[3,1,4,24,24]{4,3,2,1,0:T(8,128)S(1)} %constant_dynamic-update-slice_fusion.3), channel_id=1, source_target_pairs={{16,0},{32,16},{48,32},{17,1},{33,17},{49,33},{18,2},{34,18},{50,3... | collective-permute-start | bytes 82952 | tf_op jit(solution)/shard_map/ppermute | solution.py:20
  90.9 33.0 %slice-start = ((s8[6291456]{0:T(1024)(128)(4,1)}), s8[4194304]{0:T(1024)(128)(4,1)S(1)}, s32[]{:S(2)}) async-start(s8[6291456]{0:T(1024)(128)(4,1)} %bitcast.195), calls=%async_computation | async-start | bytes 8388608
  91.0 10.7 %collective-permute-start.16 = (f32[3,3,1,24,24]{4,3,2,1,0:T(8,128)S(1)}, f32[3,3,1,24,24]{4,3,2,1,0:T(8,128)S(1)}, u32[]{:S(2)}, u32[]{:S(2)}) collective-permute-start(f32[3,3,1,24,24]{4,3,2,1,0:T(8,128)S(1)} %get-tuple-element.15), channel_id=1, source_target_pairs={{0,1},{1,2},{2,3},{3,4},{4,5},{5,6},{6,7},{7,8},{8,9},{9,10},{10,1... | collective-permute-start | bytes 62216 | tf_op jit(solution)/shard_map/ppermute | solution.py:17
  94.6 7.0 %collective-permute-start.17 = (f32[3,3,1,24,24]{4,3,2,1,0:T(8,128)S(1)}, f32[3,3,1,24,24]{4,3,2,1,0:T(8,128)S(1)}, u32[]{:S(2)}, u32[]{:S(2)}) collective-permute-start(f32[3,3,1,24,24]{4,3,2,1,0:T(8,128)S(1)} %get-tuple-element.14), channel_id=1, source_target_pairs={{1,0},{2,1},{3,2},{4,3},{5,4},{6,5},{7,6},{8,7},{9,8},{10,9},{11,1... | collective-permute-start | bytes 62216 | tf_op jit(solution)/shard_map/ppermute | solution.py:20
  96.1 11.2 %collective-permute-start.2 = (f32[3,1,4,24,512]{4,3,2,1,0:T(8,128)S(1)}, f32[3,1,4,24,512]{4,3,2,1,0:T(8,128)S(1)}, u32[]{:S(2)}, u32[]{:S(2)}) collective-permute-start(f32[3,1,4,24,512]{4,3,2,1,0:T(8,128)S(1)} %constant_dynamic-update-slice_fusion), channel_id=1, source_target_pairs={{0,16},{16,32},{32,48},{1,17},{17,33},{33,49},{2,18},{18,34},{34,5... | collective-permute-start | bytes 1769480 | tf_op jit(solution)/shard_map/ppermute | solution.py:17
  98.0 11.0 %collective-permute-start.3 = (f32[3,1,4,24,512]{4,3,2,1,0:T(8,128)S(1)}, f32[3,1,4,24,512]{4,3,2,1,0:T(8,128)S(1)}, u32[]{:S(2)}, u32[]{:S(2)}) collective-permute-start(f32[3,1,4,24,512]{4,3,2,1,0:T(8,128)S(1)} %constant_dynamic-update-slice_fusion), channel_id=1, source_target_pairs={{16,0},{32,16},{48,32},{17,1},{33,17},{49,33},{18,2},{34,18},{50,3... | collective-permute-start | bytes 1769480 | tf_op jit(solution)/shard_map/ppermute | solution.py:20
  101.7 22.2 %slice-start.1 = ((s8[6291456]{0:T(1024)(128)(4,1)}), s8[2097152]{0:T(1024)(128)(4,1)S(1)}, s32[]{:S(2)}) async-start(s8[6291456]{0:T(1024)(128)(4,1)} %bitcast.195), calls=%async_computation.1 | async-start | bytes 4194304
  109.1 10.4 %collective-permute-start.4 = (f32[3,3,1,24,512]{4,3,2,1,0:T(8,128)S(1)}, f32[3,3,1,24,512]{4,3,2,1,0:T(8,128)S(1)}, u32[]{:S(2)}, u32[]{:S(2)}) collective-permute-start(f32[3,3,1,24,512]{4,3,2,1,0:T(8,128)S(1)} %get-tuple-element.11), channel_id=1, source_target_pairs={{0,1},{1,2},{2,3},{3,4},{4,5},{5,6},{6,7},{7,8},{8,9},{9,10},{10,1... | collective-permute-start | bytes 1327112 | tf_op jit(solution)/shard_map/ppermute | solution.py:17
  113.7 10.2 %collective-permute-start.5 = (f32[3,3,1,24,512]{4,3,2,1,0:T(8,128)S(1)}, f32[3,3,1,24,512]{4,3,2,1,0:T(8,128)S(1)}, u32[]{:S(2)}, u32[]{:S(2)}) collective-permute-start(f32[3,3,1,24,512]{4,3,2,1,0:T(8,128)S(1)} %get-tuple-element.10), channel_id=1, source_target_pairs={{1,0},{2,1},{3,2},{4,3},{5,4},{6,5},{7,6},{8,7},{9,8},{10,9},{11,1... | collective-permute-start | bytes 1327112 | tf_op jit(solution)/shard_map/ppermute | solution.py:20
  123.9 7.7 %copy-start = (f32[1,1,4,512,512]{4,3,2,1,0:T(8,128)S(1)}, f32[1,1,4,512,512]{4,3,2,1,0:T(8,128)}, u32[]{:S(2)}) copy-start(f32[1,1,4,512,512]{4,3,2,1,0:T(8,128)} %param.6) | copy-start | bytes 12582916
  138.7 11.6 %collective-permute-start.6 = (f32[1,1,4,24,512]{4,3,2,1,0:T(8,128)S(1)}, f32[1,1,4,24,512]{4,3,2,1,0:T(8,128)S(1)}, u32[]{:S(2)}, u32[]{:S(2)}) collective-permute-start(f32[1,1,4,24,512]{4,3,2,1,0:T(8,128)S(1)} %bitcast.197), channel_id=1, source_target_pairs={{0,64},{64,128},{128,192},{1,65},{65,129},{129,193},{2,66},{66,130... | collective-permute-start | bytes 589832 | tf_op jit(solution)/shard_map/ppermute | solution.py:17
  145.4 11.4 %collective-permute-start.7 = (f32[1,1,4,24,512]{4,3,2,1,0:T(8,128)S(1)}, f32[1,1,4,24,512]{4,3,2,1,0:T(8,128)S(1)}, u32[]{:S(2)}, u32[]{:S(2)}) collective-permute-start(f32[1,1,4,24,512]{4,3,2,1,0:T(8,128)S(1)} %bitcast.198), channel_id=1, source_target_pairs={{64,0},{128,64},{192,128},{65,1},{129,65},{193,129},{66,2},{130,66... | collective-permute-start | bytes 589832 | tf_op jit(solution)/shard_map/ppermute | solution.py:20
  156.8 11.2 %collective-permute-start.8 = (f32[3,1,4,24,512]{4,3,2,1,0:T(8,128)S(1)}, f32[3,1,4,24,512]{4,3,2,1,0:T(8,128)S(1)}, u32[]{:S(2)}, u32[]{:S(2)}) collective-permute-start(f32[3,1,4,24,512]{4,3,2,1,0:T(8,128)S(1)} %pad_maximum_fusion), channel_id=1, source_target_pairs={{0,16},{16,32},{32,48},{1,17},{17,33},{33,49},{2,18},{18,34},{34,5... | collective-permute-start | bytes 1769480 | tf_op jit(solution)/shard_map/ppermute | solution.py:17
  158.7 11.0 %collective-permute-start.9 = (f32[3,1,4,24,512]{4,3,2,1,0:T(8,128)S(1)}, f32[3,1,4,24,512]{4,3,2,1,0:T(8,128)S(1)}, u32[]{:S(2)}, u32[]{:S(2)}) collective-permute-start(f32[3,1,4,24,512]{4,3,2,1,0:T(8,128)S(1)} %pad_maximum_fusion), channel_id=1, source_target_pairs={{16,0},{32,16},{48,32},{17,1},{33,17},{49,33},{18,2},{34,18},{50,3... | collective-permute-start | bytes 1769480 | tf_op jit(solution)/shard_map/ppermute | solution.py:20
  169.9 9.2 %collective-permute-start.10 = (f32[3,3,1,24,512]{4,3,2,1,0:T(8,128)S(1)}, f32[3,3,1,24,512]{4,3,2,1,0:T(8,128)S(1)}, u32[]{:S(2)}, u32[]{:S(2)}) collective-permute-start(f32[3,3,1,24,512]{4,3,2,1,0:T(8,128)S(1)} %get-tuple-element.9), channel_id=1, source_target_pairs={{0,1},{1,2},{2,3},{3,4},{4,5},{5,6},{6,7},{7,8},{8,9},{9,10},{10,1... | collective-permute-start | bytes 1327112 | tf_op jit(solution)/shard_map/ppermute | solution.py:17
  173.3 10.2 %collective-permute-start.11 = (f32[3,3,1,24,512]{4,3,2,1,0:T(8,128)S(1)}, f32[3,3,1,24,512]{4,3,2,1,0:T(8,128)S(1)}, u32[]{:S(2)}, u32[]{:S(2)}) collective-permute-start(f32[3,3,1,24,512]{4,3,2,1,0:T(8,128)S(1)} %get-tuple-element.8), channel_id=1, source_target_pairs={{1,0},{2,1},{3,2},{4,3},{5,4},{6,5},{7,6},{8,7},{9,8},{10,9},{11,1... | collective-permute-start | bytes 1327112 | tf_op jit(solution)/shard_map/ppermute | solution.py:20
  190.8 8.3 %collective-permute-start.18 = (f32[1,1,4,24,24]{4,3,2,1,0:T(8,128)S(1)}, f32[1,1,4,24,24]{4,3,2,1,0:T(8,128)S(1)}, u32[]{:S(2)}, u32[]{:S(2)}) collective-permute-start(f32[1,1,4,24,24]{4,3,2,1,0:T(8,128)S(1)} %bitcast.203), channel_id=1, source_target_pairs={{0,64},{64,128},{128,192},{1,65},{65,129},{129,193},{2,66},{66,130... | collective-permute-start | bytes 27656 | tf_op jit(solution)/shard_map/ppermute | solution.py:17
  196.9 7.1 %collective-permute-start.19 = (f32[1,1,4,24,24]{4,3,2,1,0:T(8,128)S(1)}, f32[1,1,4,24,24]{4,3,2,1,0:T(8,128)S(1)}, u32[]{:S(2)}, u32[]{:S(2)}) collective-permute-start(f32[1,1,4,24,24]{4,3,2,1,0:T(8,128)S(1)} %bitcast.204), channel_id=1, source_target_pairs={{64,0},{128,64},{192,128},{65,1},{129,65},{193,129},{66,2},{130,66... | collective-permute-start | bytes 27656 | tf_op jit(solution)/shard_map/ppermute | solution.py:20
  204.0 6.5 %collective-permute-start.20 = (f32[3,1,4,24,24]{4,3,2,1,0:T(8,128)S(1)}, f32[3,1,4,24,24]{4,3,2,1,0:T(8,128)S(1)}, u32[]{:S(2)}, u32[]{:S(2)}) collective-permute-start(f32[3,1,4,24,24]{4,3,2,1,0:T(8,128)S(1)} %pad_maximum_fusion.26), channel_id=1, source_target_pairs={{0,16},{16,32},{32,48},{1,17},{17,33},{33,49},{2,18},{18,34},{34,5... | collective-permute-start | bytes 82952 | tf_op jit(solution)/shard_map/ppermute | solution.py:17
  205.9 6.3 %collective-permute-start.21 = (f32[3,1,4,24,24]{4,3,2,1,0:T(8,128)S(1)}, f32[3,1,4,24,24]{4,3,2,1,0:T(8,128)S(1)}, u32[]{:S(2)}, u32[]{:S(2)}) collective-permute-start(f32[3,1,4,24,24]{4,3,2,1,0:T(8,128)S(1)} %pad_maximum_fusion.26), channel_id=1, source_target_pairs={{16,0},{32,16},{48,32},{17,1},{33,17},{49,33},{18,2},{34,18},{50,3... | collective-permute-start | bytes 82952 | tf_op jit(solution)/shard_map/ppermute | solution.py:20
  212.3 8.1 %collective-permute-start.22 = (f32[3,3,1,24,24]{4,3,2,1,0:T(8,128)S(1)}, f32[3,3,1,24,24]{4,3,2,1,0:T(8,128)S(1)}, u32[]{:S(2)}, u32[]{:S(2)}) collective-permute-start(f32[3,3,1,24,24]{4,3,2,1,0:T(8,128)S(1)} %get-tuple-element.13), channel_id=1, source_target_pairs={{0,1},{1,2},{2,3},{3,4},{4,5},{5,6},{6,7},{7,8},{8,9},{9,10},{10,1... | collective-permute-start | bytes 62216 | tf_op jit(solution)/shard_map/ppermute | solution.py:17
  218.0 6.6 %collective-permute-start.23 = (f32[3,3,1,24,24]{4,3,2,1,0:T(8,128)S(1)}, f32[3,3,1,24,24]{4,3,2,1,0:T(8,128)S(1)}, u32[]{:S(2)}, u32[]{:S(2)}) collective-permute-start(f32[3,3,1,24,24]{4,3,2,1,0:T(8,128)S(1)} %get-tuple-element.12), channel_id=1, source_target_pairs={{1,0},{2,1},{3,2},{4,3},{5,4},{6,5},{7,6},{8,7},{9,8},{10,9},{11,1... | collective-permute-start | bytes 62216 | tf_op jit(solution)/shard_map/ppermute | solution.py:20
where the time goes:
time: 301 us; the launch traced here: 299 us
  starting transfers between devices  74.5 us (25%)
  blocking collectives  71.5 us (24%)
  local copies, waits for them, and re-layouts  69.3 us (23%)
  waiting for transfers between devices  54 us (18%)
  matrix products  28 us (9%)
    psum x1, blocking collectives, per_device(): column = lax.psum(jnp.sum(partials, axis=0), 'gz')  71.5 us
    unnamed x32, local copies, waits for them, and re-layouts  62.8 us
    ppermute x12, starting transfers between devices, padded_2(): lax.ppermute(lax.slice_in_dim(block, block.shape[dim] - width, None, axis...  49.2 us
    ppermute x12, waiting for transfers between devices, padded_2(): lax.ppermute(lax.slice_in_dim(block, 0, width, axis=dim), axis, backward)  31.5 us
    ppermute x12, starting transfers between devices, padded_2(): lax.ppermute(lax.slice_in_dim(block, 0, width, axis=dim), axis, backward)  25.3 us
    ppermute x12, waiting for transfers between devices, padded_2(): lax.ppermute(lax.slice_in_dim(block, block.shape[dim] - width, None, axis...  22.4 us
  transfers between devices with their start and end apart: 24, of which 17 were waited for; matrix products, arithmetic and copies ran while one was open for 24% of the time, Pallas kernels for 0%

commit v1 on v0

v1 whole, which is shorter than its diff:
```python
import functools

import jax
import jax.numpy as jnp
from jax import lax
from jax.experimental import pallas as pl
from jax.experimental.pallas import tpu as pltpu
from jax.sharding import PartitionSpec as P

MESH = pl.DeviceIdType.MESH
HIGHEST = lax.Precision.HIGHEST
OMEGA_FINE = 2.0 / 3.0
OMEGA_COARSE = 1.0
EPSILON = 1e-06
LANES = 128


def dot_nt(left, right, precision=None):
    return lax.dot_general(
        left, right, (((1,), (1,)), ((), ())), precision=precision, preferred_element_type=jnp.float32
    )


def dot_nn(left, right, precision=None):
    return lax.dot_general(
        left, right, (((1,), (0,)), ((), ())), precision=precision, preferred_element_type=jnp.float32
    )


def split(value):
    high = value.astype(jnp.bfloat16).astype(jnp.float32)
    return jnp.concatenate([high, value - high], axis=0).astype(jnp.bfloat16)


def fold(value):
    half = value.shape[0] // 2
    return value[:half] + value[half:]


def split_into(source, high_ref, low_ref, rows, step):
    for start in range(0, rows, step):
        part = source[pl.ds(start, step)]
        high = part.astype(jnp.bfloat16)
        high_ref[pl.ds(start, step)] = high
        low_ref[pl.ds(start, step)] = (part - high.astype(jnp.float32)).astype(jnp.bfloat16)


def kernel(
    sizes,
    near_hbm,
    diag_hbm,
    face_hbm,
    rows_hbm,
    modes_hbm,
    coarse_out,
    column_out,
    near_x,
    near_y,
    near_z,
    smooth_x,
    smooth_y,
    smooth_z,
    diag_in,
    face_in,
    rows_in,
    modes_in,
    diag_high,
    diag_low,
    face_high,
    face_low,
    selector,
    product,
    diagonal,
    reach,
    own_block,
    modes_pack,
    modes_halo,
    right,
    left,
    part,
    gathered,
    load_sem,
    diag_sem,
    face_sem,
    near_send,
    near_recv,
    smooth_send,
    smooth_recv,
    modes_send,
    modes_recv,
    result_send,
    result_recv,
    sum_send,
    sum_recv,
):
    n_x, n_y, n_z = sizes
    count, modes, dofs = product.shape
    face = face_in.shape[2]
    last = count - 1
    gx, gy, gz = lax.axis_index("gx"), lax.axis_index("gy"), lax.axis_index("gz")
    has = [gx > 0, gx < n_x - 1, gy > 0, gy < n_y - 1, gz > 0, gz < n_z - 1]
    target = [
        {"gx": gx - 1},
        {"gx": gx + 1},
        {"gy": gy - 1},
        {"gy": gy + 1},
        {"gz": gz - 1},
        {"gz": gz + 1},
    ]
    passes_up = (gy == 2) & has[1]
    passes_down = (gy == 1) & has[0]
    pass_up = {"gx": gx + 1, "gy": gy - 1}
    pass_down = {"gx": gx - 1, "gy": gy + 1}
    peers = [lax.rem(gz + step, n_z) for step in range(1, n_z)]

    loads = [
        pltpu.make_async_copy(near_hbm.at[0, 0], near_z.at[pl.ds(1, count)], load_sem.at[0]),
        pltpu.make_async_copy(rows_hbm.at[0, 0], rows_in, load_sem.at[1]),
        pltpu.make_async_copy(modes_hbm.at[0, 0], modes_in, load_sem.at[2]),
    ]
    for load in loads:
        load.start()

    def load_diag(at):
        return pltpu.make_async_copy(diag_hbm.at[0, 0, at], diag_in.at[at], diag_sem.at[at])

    def load_face(at):
        return pltpu.make_async_copy(face_hbm.at[0, 0, at], face_in.at[at], face_sem.at[at])

    for at in range(count):
        load_diag(at).start()
    for at in range(count):
        load_face(at).start()

    right[...] = jnp.zeros_like(right)

    barrier = pltpu.get_barrier_semaphore()
    for side in range(4):

        @pl.when(has[side])
        def _(side=side):
            pl.semaphore_signal(barrier, inc=1, device_id=target[side], device_id_type=MESH)

    @pl.when(passes_up)
    def _():
        pl.semaphore_signal(barrier, inc=1, device_id=pass_up, device_id_type=MESH)

    @pl.when(passes_down)
    def _():
        pl.semaphore_signal(barrier, inc=1, device_id=pass_down, device_id_type=MESH)

    for peer in peers:
        pl.semaphore_signal(barrier, inc=1, device_id={"gz": peer}, device_id_type=MESH)

    for side in range(2):

        @pl.when(jnp.logical_not(has[side]))
        def _(side=side):
            near_x[side] = jnp.zeros_like(near_x[side])
            smooth_x[side] = jnp.zeros_like(smooth_x[side])

        @pl.when(jnp.logical_not(has[2 + side]))
        def _(side=side):
            near_y[side] = jnp.zeros_like(near_y[side])
            smooth_y[side] = jnp.zeros_like(smooth_y[side])

        @pl.when(jnp.logical_not(has[4 + side]))
        def _(side=side):
            near_z[side * (count + 1)] = jnp.zeros((modes, dofs), jnp.float32)
            smooth_z[side * (count + 1)] = jnp.zeros((modes, dofs), jnp.float32)

    for side in range(6):

        @pl.when(jnp.logical_not(has[side]))
        def _(side=side):
            modes_halo[side] = jnp.zeros_like(modes_halo[side])

    loads[2].wait()
    pieces = [modes_in[at].T for at in range(count)]
    pieces.append(jnp.zeros((modes, LANES - count * modes), jnp.float32))
    modes_pack[...] = jnp.concatenate(pieces, axis=1)
    loads[1].wait()

    def build_selector(at, carry):
        for side in range(6):
            chosen = rows_in[at, pl.ds(side, 1), :]
            for start in range(0, dofs, LANES):
                row = lax.broadcasted_iota(jnp.int32, (LANES, face), 0) + start
                hit = jnp.where(row == chosen, 1.0, 0.0).astype(jnp.bfloat16)
                selector[at, pl.ds(start, LANES), pl.ds(side * face, face)] = hit
        return carry

    lax.fori_loop(0, count, build_selector, 0)
    loads[0].wait()

    met = n_z - 1
    for flag in has[:4] + [passes_up | passes_down]:
        met = met + flag.astype(jnp.int32)
    pl.semaphore_wait(barrier, met)

    def halo(bufs, sems, side, at, landing):
        buf_x, buf_y, buf_z = bufs
        send, recv = sems
        if side < 2:
            dst = buf_x.at[landing, at]
        elif side < 4:
            dst = buf_y.at[landing - 2, at]
        else:
            dst = buf_z.at[(landing - 4) * (count + 1)]
        return pltpu.make_async_remote_copy(
            src_ref=buf_z.at[at + 1],
            dst_ref=dst,
            send_sem=send.at[side, at],
            recv_sem=recv.at[landing, at],
            device_id=target[side],
            device_id_type=MESH,
        )

    def passed(bufs, sems, up, at):
        buf_x, buf_y, _ = bufs
        send, recv = sems
        landing = 0 if up else 1
        return pltpu.make_async_remote_copy(
            src_ref=buf_y.at[landing, at],
            dst_ref=buf_x.at[landing, at],
            send_sem=send.at[6, at],
            recv_sem=recv.at[landing, at],
            device_id=pass_up if up else pass_down,
            device_id_type=MESH,
        )

    direct = [has[0] & (gy != 2), has[1] & (gy != 1), has[2], has[3], has[4], has[5]]

    def send_halo(bufs, sems, at):
        for side in (2, 3, 0, 1):

            @pl.when(direct[side])
            def _(side=side):
                halo(bufs, sems, side, at, side ^ 1).start()

        @pl.when(has[4] & (at == 0))
        def _():
            halo(bufs, sems, 4, at, 5).start()

        @pl.when(has[5] & (at == last))
        def _():
            halo(bufs, sems, 5, at, 4).start()

    def wait_y_and_pass(bufs, sems, at):
        for side in (2, 3):

            @pl.when(has[side])
            def _(side=side):
                halo(bufs, sems, side, at, side).wait_recv()

        @pl.when(passes_up)
        def _():
            passed(bufs, sems, True, at).start()

        @pl.when(passes_down)
        def _():
            passed(bufs, sems, False, at).start()

    def wait_xz(bufs, sems, at):
        for side in (0, 1):

            @pl.when(has[side])
            def _(side=side):
                halo(bufs, sems, side, at, side).wait_recv()

        @pl.when(has[4] & (at == 0))
        def _():
            halo(bufs, sems, 4, last, 4).wait_recv()

        @pl.when(has[5] & (at == last))
        def _():
            halo(bufs, sems, 5, 0, 5).wait_recv()

    def wait_sent(bufs, sems, at):
        for side in (2, 3, 0, 1):

            @pl.when(direct[side])
            def _(side=side):
                halo(bufs, sems, side, at, side ^ 1).wait_send()

        @pl.when(has[4] & (at == 0))
        def _():
            halo(bufs, sems, 4, at, 5).wait_send()

        @pl.when(has[5] & (at == last))
        def _():
            halo(bufs, sems, 5, at, 4).wait_send()

        @pl.when(passes_up)
        def _():
            passed(bufs, sems, True, at).wait_send()

        @pl.when(passes_down)
        def _():
            passed(bufs, sems, False, at).wait_send()

    near_bufs, near_sems = (near_x, near_y, near_z), (near_send, near_recv)
    smooth_bufs, smooth_sems = (smooth_x, smooth_y, smooth_z), (smooth_send, smooth_recv)

    def send_near(at, carry):
        send_halo(near_bufs, near_sems, at)
        return carry

    lax.fori_loop(0, count, send_near, 0)

    def modes_copy(side, landing):
        return pltpu.make_async_remote_copy(
            src_ref=modes_pack,
            dst_ref=modes_halo.at[landing],
            send_sem=modes_send.at[side],
            recv_sem=modes_recv.at[landing],
            device_id=target[side],
            device_id_type=MESH,
        )

    for side in range(6):

        @pl.when(has[side])
        def _(side=side):
            modes_copy(side, side ^ 1).start()

    def own_product(at, carry):
        load_diag(at).wait()
        split_into(diag_in.at[at], diag_high.at[at], diag_low.at[at], dofs, 64)
        here = []
        for start in range(0, dofs, LANES):
            block = diag_in[at, pl.ds(start, LANES), pl.ds(start, LANES)]
            row = lax.broadcasted_iota(jnp.int32, (LANES, LANES), 0)
            col = lax.broadcasted_iota(jnp.int32, (LANES, LANES), 1)
            here.append(jnp.sum(jnp.where(row == col, block, 0.0), axis=0, keepdims=True))
        diagonal[at] = jnp.concatenate(here, axis=1)
        value = split(near_z[at + 1])
        product[at] = fold(dot_nt(value, diag_high[at]) + dot_nt(value, diag_low[at]))
        return carry

    lax.fori_loop(0, count, own_product, 0)
    wait_y_and_pass(near_bufs, near_sems, 0)

    def smooth(at, carry):
        load_face(at).wait()
        for side in range(6):
            split_into(
                face_in.at[at, side], face_high.at[at, side], face_low.at[at, side], face, 64
            )
        wait_xz(near_bufs, near_sems, at)

        @pl.when(at < last)
        def _():
            wait_y_and_pass(near_bufs, near_sems, at + 1)

        terms = []
        for side in range(6):
            if side < 2:
                value = near_x[side, at]
            elif side < 4:
                value = near_y[side - 2, at]
            else:
                value = near_z[at + 2 * (side - 4)]
            value = split(value)
            terms.append(
                fold(dot_nt(value, face_high[at, side]) + dot_nt(value, face_low[at, side]))
            )
        terms = split(jnp.concatenate(terms, axis=1))
        total = product[at] + fold(dot_nt(terms, selector[at]))
        smooth_z[at + 1] = near_z[at + 1] - OMEGA_FINE * total / diagonal[at]
        send_halo(smooth_bufs, smooth_sems, at)

        @pl.when(at > 0)
        def _():
            wait_y_and_pass(smooth_bufs, smooth_sems, at - 1)

        return carry

    lax.fori_loop(0, count, smooth, 0)

    def coarse_local(at, carry):
        value = split(smooth_z[at + 1])
        applied = split(fold(dot_nt(value, diag_high[at]) + dot_nt(value, diag_low[at])))
        own = fold(dot_nt(value, applied))
        own_block[at] = own[:, :modes] + own[:, modes:]
        picked = dot_nn(value, selector[at]).astype(jnp.bfloat16)
        for side in range(6):
            here = picked[:, side * face : (side + 1) * face]
            reach[at, side] = split(
                fold(dot_nn(here, face_high[at, side]) + dot_nn(here, face_low[at, side]))
            )

        @pl.when(at == 1)
        def _():
            wait_y_and_pass(smooth_bufs, smooth_sems, last)

        return carry

    lax.fori_loop(0, count, coarse_local, 0)

    for side in range(6):

        @pl.when(has[side])
        def _(side=side):
            modes_copy(side, side).wait_recv()

    own_modes = modes_pack[...]
    zero_block = jnp.zeros((modes, modes), jnp.float32)

    def lane_block(value, at):
        return value[:, at * modes : (at + 1) * modes]

    along_z = (
        [lane_block(modes_halo[4], last)]
        + [lane_block(own_modes, at) for at in range(count)]
        + [lane_block(modes_halo[5], 0)]
    )
    around = []
    for at in range(count):
        sides = [lane_block(modes_halo[side], at) for side in range(4)]
        around.append(
            jnp.concatenate([along_z[at + 1]] + sides + [along_z[at], along_z[at + 2]], axis=1)
        )

    smoothed_t, through = [], []
    for at in range(count):
        wait_xz(smooth_bufs, smooth_sems, at)
        blocks = [own_block[at]]
        for side in range(6):
            if side < 2:
                value = smooth_x[side, at]
            elif side < 4:
                value = smooth_y[side - 2, at]
            else:
                value = smooth_z[at + 2 * (side - 4)]
            lateral = fold(dot_nt(reach[at, side], split(value)))
            blocks.append(lateral[:, :modes] + lateral[:, modes:])
        coarse = jnp.concatenate(blocks, axis=1)
        coarse_out[at] = coarse
        scale = dot_nt(jnp.ones_like(coarse), jnp.abs(coarse), HIGHEST) + EPSILON
        applied = dot_nt(around[at], coarse, HIGHEST)
        result = along_z[at + 1] - OMEGA_COARSE * applied / scale
        smoothed_t.append(result)
        through.append(dot_nn(result, coarse, HIGHEST))

    right_rows = [1, 2, 3, 4, 0, 0]
    filler = jnp.zeros((modes, LANES - count * modes), jnp.float32)
    right[pl.ds(0, modes), pl.ds(0, LANES)] = jnp.concatenate(smoothed_t + [filler], axis=1)

    def result_copy(side, landing):
        return pltpu.make_async_remote_copy(
            src_ref=right.at[pl.ds(0, modes), pl.ds(0, LANES)],
            dst_ref=right.at[
                pl.ds(right_rows[landing] * modes, modes), pl.ds((landing + 1) * LANES, LANES)
            ],
            send_sem=result_send.at[side],
            recv_sem=result_recv.at[landing],
            device_id=target[side],
            device_id_type=MESH,
        )

    for side in range(6):

        @pl.when(has[side])
        def _(side=side):
            result_copy(side, side ^ 1).start()

    def block_of(at, which):
        return lane_block(through[at], which)

    centre = []
    for at in range(count):
        value = block_of(at, 0)
        if at < last:
            value = value + block_of(at + 1, 5)
        if at > 0:
            value = value + block_of(at - 1, 6)
        centre.append(value)
    left[:, pl.ds(0, LANES)] = jnp.concatenate(centre + [filler], axis=1)
    for side in range(4):
        pieces = [block_of(at, side + 1) for at in range(count)]
        left[:, pl.ds((side + 1) * LANES, LANES)] = jnp.concatenate(pieces + [filler], axis=1)
    low = [zero_block] * last + [block_of(0, 5)]
    left[:, pl.ds(5 * LANES, LANES)] = jnp.concatenate(low + [filler], axis=1)
    high = [block_of(last, 6)] + [zero_block] * last
    left[:, pl.ds(6 * LANES, LANES)] = jnp.concatenate(high + [filler], axis=1)

    for side in range(6):

        @pl.when(has[side])
        def _(side=side):
            result_copy(side, side).wait_recv()

    part[...] = dot_nt(left[...], right[...], HIGHEST)
    gathered[gz] = part[...]
    shares = [
        pltpu.make_async_remote_copy(
            src_ref=part,
            dst_ref=gathered.at[gz],
            send_sem=sum_send.at[at],
            recv_sem=sum_recv.at[at],
            device_id={"gz": peer},
            device_id_type=MESH,
        )
        for at, peer in enumerate(peers)
    ]
    for share in shares:
        share.start()

    def finish(at, carry):
        wait_sent(near_bufs, near_sems, at)
        wait_sent(smooth_bufs, smooth_sems, at)
        return carry

    lax.fori_loop(0, count, finish, 0)
    for side in range(6):

        @pl.when(has[side])
        def _(side=side):
            modes_copy(side, side ^ 1).wait_send()
            result_copy(side, side ^ 1).wait_send()

    for share in shares:
        share.wait()
    total = gathered[0]
    for at in range(1, n_z):
        total = total + gathered[at]
    column_out[...] = total[:, : 5 * modes]


def per_device(sizes, near_modes, diag_blocks, face_blocks, face_rows, coarse_modes):
    count, modes, dofs = near_modes.shape[2:]
    face = face_blocks.shape[4]
    n_z = sizes[2]
    any_space = pl.BlockSpec(memory_space=pl.ANY)
    vmem = pl.BlockSpec(memory_space=pltpu.VMEM)
    f32, bf16 = jnp.float32, jnp.bfloat16
    dma = pltpu.SemaphoreType.DMA
    coarse_one, column = pl.pallas_call(
        functools.partial(kernel, sizes),
        out_shape=(
            jax.ShapeDtypeStruct((count, modes, 7 * modes), f32),
            jax.ShapeDtypeStruct((modes, 5 * modes), f32),
        ),
        in_specs=[any_space] * 5,
        out_specs=(vmem, vmem),
        scratch_shapes=[
            pltpu.VMEM((2, count, modes, dofs), f32),
            pltpu.VMEM((2, count, modes, dofs), f32),
            pltpu.VMEM((count + 2, modes, dofs), f32),
            pltpu.VMEM((2, count, modes, dofs), f32),
            pltpu.VMEM((2, count, modes, dofs), f32),
            pltpu.VMEM((count + 2, modes, dofs), f32),
            pltpu.VMEM((count, dofs, dofs), f32),
            pltpu.VMEM((count, 6, face, dofs), f32),
            pltpu.VMEM((count, 6, face), jnp.int32),
            pltpu.VMEM((count, modes, modes), f32),
            pltpu.VMEM((count, dofs, dofs), bf16),
            pltpu.VMEM((count, dofs, dofs), bf16),
            pltpu.VMEM((count, 6, face, dofs), bf16),
            pltpu.VMEM((count, 6, face, dofs), bf16),
            pltpu.VMEM((count, dofs, 6 * face), bf16),
            pltpu.VMEM((count, modes, dofs), f32),
            pltpu.VMEM((count, 1, dofs), f32),
            pltpu.VMEM((count, 6, 2 * modes, dofs), bf16),
            pltpu.VMEM((count, modes, modes), f32),
            pltpu.VMEM((modes, LANES), f32),
            pltpu.VMEM((6, modes, LANES), f32),
            pltpu.VMEM((LANES, 7 * LANES), f32),
            pltpu.VMEM((modes, 7 * LANES), f32),
            pltpu.VMEM((modes, LANES), f32),
            pltpu.VMEM((n_z, modes, LANES), f32),
            dma((3,)),
            dma((count,)),
            dma((count,)),
            dma((7, count)),
            dma((6, count)),
            dma((7, count)),
            dma((6, count)),
            dma((6,)),
            dma((6,)),
            dma((6,)),
            dma((6,)),
            dma((n_z - 1,)),
            dma((n_z - 1,)),
        ],
        compiler_params=pltpu.CompilerParams(
            collective_id=0, has_side_effects=True, vmem_limit_bytes=48 * 2**20
        ),
        cost_estimate=pl.CostEstimate(flops=2 * 10**9, bytes_accessed=11 * 10**6, transcendentals=0),
    )(near_modes, diag_blocks, face_blocks, face_rows, coarse_modes)
    return coarse_one[None, None], column[None, None]


def solution(mesh):
    placed = (
        P("gx", "gy", "gz", None, None),
        P("gx", "gy", "gz", None, None),
        P("gx", "gy", "gz", None, None, None),
        P("gx", "gy", "gz", None, None),
        P("gx", "gy", "gz", None, None),
    )
    sizes = tuple(mesh.shape[axis] for axis in ("gx", "gy", "gz"))
    return jax.shard_map(
        functools.partial(per_device, sizes),
        mesh=mesh,
        in_specs=placed,
        out_specs=(P("gx", "gy", "gz", None, None), P("gx", "gy", None, None)),
        check_vma=False,
    )
```

time: 301 us -> 55.5 us (0.18)
  the two profiles are of different devices: /device:TPU:32 before, /device:TPU:1 now
where the time goes in v1:
time: 55.5 us; the launch traced here: 55.3 us
  Pallas kernels  48.8 us (88%)
  local copies, waits for them, and re-layouts  5.86 us (11%)
  between operations  0.64 us (1%)
    pallas_call x1, Pallas kernels, per_device(): pl.pallas_call(functools.partial(kernel, sizes), out_shape=(jax.ShapeDtyp...  48.8 us
    unnamed x9, local copies, waits for them, and re-layouts  5.86 us

profile of v1, /device:TPU:1, one launch (start us, length us, event | category | flops | bytes accessed | tf_op | source)
XLA Modules:
  0.0 55.3 jit_solution(14614418918258458421)
XLA Ops:
  0.6 0.7 %copy.7.rows_hbm = s32[1,1,4,6,128]{4,3,2,1,0:T(8,128)S(1)} copy(s32[1,1,4,6,128]{4,2,3,1,0:T(4,128)} %param.8) | data formatting | bytes 24576 | tf_op args[3]
  1.3 0.0 copy-start
  1.3 2.2 %copy-done = f32[1,1,4,512,512]{4,3,2,1,0:T(8,128)S(1)} copy-done((f32[1,1,4,512,512]{4,3,2,1,0:T(8,128)S(1)}, f32[1,1,4,512,512]{4,3,2,1,0:T(8,128)}, u32[]{:S(2)}) %copy-start) | copy-done | bytes 4194328
  3.5 0.0 copy-start.1
  3.5 0.9 %copy-done.1 = f32[1,1,4,24,512]{4,3,2,1,0:T(8,128)S(1)} copy-done((f32[1,1,4,24,512]{4,3,2,1,0:T(8,128)S(1)}, f32[1,1,4,24,512]{4,3,2,1,0:T(8,128)}, u32[]{:S(2)}) %copy-start.1) | copy-done | bytes 196632
  4.5 0.0 copy-start.2
  4.5 0.8 %copy-done.2 = f32[1,1,4,24,24]{4,3,2,1,0:T(8,128)S(1)} copy-done((f32[1,1,4,24,24]{4,3,2,1,0:T(8,128)S(1)}, f32[1,1,4,24,24]{4,3,2,1,0:T(8,128)}, u32[]{:S(2)}) %copy-start.2) | copy-done | bytes 9240
  5.3 48.8 %shard_map.68 = (f32[4,24,168]{2,1,0:T(8,128)S(1)}, f32[24,120]{1,0:T(8,128)S(1)}) custom-call(f32[1,1,4,24,512]{4,3,2,1,0:T(8,128)S(1)} %copy-done.1, f32[1,1,4,512,512]{4,3,2,1,0:T(8,128)S(1)} %copy-done, f32[1,1,4,6,128,512]{5,4,3,2,1,0:T(8,128)} %face_hbm.1, s32[1,1,4,6,128]{4,3,2,1,0:T(8,128)S(1)} %copy.7.rows_hbm, f32[1,1,4,24,24]{4,3,2,1,0:T(8,128)S(1)} %copy-done.2), custom_call_target="tpu_custom_call" | custom-call | flops 2000000000 | bytes 11000000 | tf_op jit(solution)/shard_map/pallas_call | solution.py:539
  54.0 0.6 %copy.10 = f32[1,1,4,24,168]{4,3,2,1,0:T(8,128)} copy(f32[1,1,4,24,168]{4,3,2,1,0:T(8,128)S(1)} %bitcast.2) | data formatting | bytes 129024
  54.7 0.6 %copy.11 = f32[1,1,24,120]{3,2,1,0:T(8,128)} copy(f32[1,1,24,120]{3,2,1,0:T(8,128)S(1)} %bitcast.3) | data formatting | bytes 23040
Async XLA Ops:
  1.3 2.2 %copy-start = (f32[1,1,4,512,512]{4,3,2,1,0:T(8,128)S(1)}, f32[1,1,4,512,512]{4,3,2,1,0:T(8,128)}, u32[]{:S(2)}) copy-start(f32[1,1,4,512,512]{4,3,2,1,0:T(8,128)} %diag_hbm.1) | copy-start | bytes 12582916
  3.5 0.9 %copy-start.1 = (f32[1,1,4,24,512]{4,3,2,1,0:T(8,128)S(1)}, f32[1,1,4,24,512]{4,3,2,1,0:T(8,128)}, u32[]{:S(2)}) copy-start(f32[1,1,4,24,512]{4,3,2,1,0:T(8,128)} %near_hbm.1) | copy-start | bytes 589828
  4.5 0.8 %copy-start.2 = (f32[1,1,4,24,24]{4,3,2,1,0:T(8,128)S(1)}, f32[1,1,4,24,24]{4,3,2,1,0:T(8,128)}, u32[]{:S(2)}) copy-start(f32[1,1,4,24,24]{4,3,2,1,0:T(8,128)} %modes_hbm.1) | copy-start | bytes 27652

commit v2 on v1

--- a/solution.py
+++ b/solution.py
@@ -107,10 +107,6 @@
         {"gz": gz - 1},
         {"gz": gz + 1},
     ]
-    passes_up = (gy == 2) & has[1]
-    passes_down = (gy == 1) & has[0]
-    pass_up = {"gx": gx + 1, "gy": gy - 1}
-    pass_down = {"gx": gx - 1, "gy": gy + 1}
     peers = [lax.rem(gz + step, n_z) for step in range(1, n_z)]
 
     loads = [
@@ -141,14 +137,6 @@
         def _(side=side):
             pl.semaphore_signal(barrier, inc=1, device_id=target[side], device_id_type=MESH)
 
-    @pl.when(passes_up)
-    def _():
-        pl.semaphore_signal(barrier, inc=1, device_id=pass_up, device_id_type=MESH)
-
-    @pl.when(passes_down)
-    def _():
-        pl.semaphore_signal(barrier, inc=1, device_id=pass_down, device_id_type=MESH)
-
     for peer in peers:
         pl.semaphore_signal(barrier, inc=1, device_id={"gz": peer}, device_id_type=MESH)
 
@@ -183,7 +171,7 @@
 
     def build_selector(at, carry):
         for side in range(6):
-            chosen = rows_in[at, pl.ds(side, 1), :]
+            chosen = rows_in[side, pl.ds(at, 1), :]
             for start in range(0, dofs, LANES):
                 row = lax.broadcasted_iota(jnp.int32, (LANES, face), 0) + start
                 hit = jnp.where(row == chosen, 1.0, 0.0).astype(jnp.bfloat16)
@@ -194,7 +182,7 @@
     loads[0].wait()
 
     met = n_z - 1
-    for flag in has[:4] + [passes_up | passes_down]:
+    for flag in has[:4]:
         met = met + flag.astype(jnp.int32)
     pl.semaphore_wait(barrier, met)
 
@@ -216,25 +204,10 @@
             device_id_type=MESH,
         )
 
-    def passed(bufs, sems, up, at):
-        buf_x, buf_y, _ = bufs
-        send, recv = sems
-        landing = 0 if up else 1
-        return pltpu.make_async_remote_copy(
-            src_ref=buf_y.at[landing, at],
-            dst_ref=buf_x.at[landing, at],
-            send_sem=send.at[6, at],
-            recv_sem=recv.at[landing, at],
-            device_id=pass_up if up else pass_down,
-            device_id_type=MESH,
-        )
-
-    direct = [has[0] & (gy != 2), has[1] & (gy != 1), has[2], has[3], has[4], has[5]]
-
     def send_halo(bufs, sems, at):
         for side in (2, 3, 0, 1):
 
-            @pl.when(direct[side])
+            @pl.when(has[side])
             def _(side=side):
                 halo(bufs, sems, side, at, side ^ 1).start()
 
@@ -246,21 +219,13 @@
         def _():
             halo(bufs, sems, 5, at, 4).start()
 
-    def wait_y_and_pass(bufs, sems, at):
+    def wait_y(bufs, sems, at):
         for side in (2, 3):
 
             @pl.when(has[side])
             def _(side=side):
                 halo(bufs, sems, side, at, side).wait_recv()
 
-        @pl.when(passes_up)
-        def _():
-            passed(bufs, sems, True, at).start()
-
-        @pl.when(passes_down)
-        def _():
-            passed(bufs, sems, False, at).start()
-
     def wait_xz(bufs, sems, at):
         for side in (0, 1):
 
@@ -279,7 +244,7 @@
     def wait_sent(bufs, sems, at):
         for side in (2, 3, 0, 1):
 
-            @pl.when(direct[side])
+            @pl.when(has[side])
             def _(side=side):
                 halo(bufs, sems, side, at, side ^ 1).wait_send()
 
@@ -290,14 +255,6 @@
         @pl.when(has[5] & (at == last))
         def _():
             halo(bufs, sems, 5, at, 4).wait_send()
-
-        @pl.when(passes_up)
-        def _():
-            passed(bufs, sems, True, at).wait_send()
-
-        @pl.when(passes_down)
-        def _():
-            passed(bufs, sems, False, at).wait_send()
 
     near_bufs, near_sems = (near_x, near_y, near_z), (near_send, near_recv)
     smooth_bufs, smooth_sems = (smooth_x, smooth_y, smooth_z), (smooth_send, smooth_recv)
@@ -339,7 +296,6 @@
         return carry
 
     lax.fori_loop(0, count, own_product, 0)
-    wait_y_and_pass(near_bufs, near_sems, 0)
 
     def smooth(at, carry):
         load_face(at).wait()
@@ -347,11 +303,8 @@
             split_into(
                 face_in.at[at, side], face_high.at[at, side], face_low.at[at, side], face, 64
             )
+        wait_y(near_bufs, near_sems, at)
         wait_xz(near_bufs, near_sems, at)
-
-        @pl.when(at < last)
-        def _():
-            wait_y_and_pass(near_bufs, near_sems, at + 1)
 
         terms = []
         for side in range(6):
@@ -369,11 +322,6 @@
         total = product[at] + fold(dot_nt(terms, selector[at]))
         smooth_z[at + 1] = near_z[at + 1] - OMEGA_FINE * total / diagonal[at]
         send_halo(smooth_bufs, smooth_sems, at)
-
-        @pl.when(at > 0)
-        def _():
-            wait_y_and_pass(smooth_bufs, smooth_sems, at - 1)
-
         return carry
 
     lax.fori_loop(0, count, smooth, 0)
@@ -389,11 +337,6 @@
             reach[at, side] = split(
                 fold(dot_nn(here, face_high[at, side]) + dot_nn(here, face_low[at, side]))
             )
-
-        @pl.when(at == 1)
-        def _():
-            wait_y_and_pass(smooth_bufs, smooth_sems, last)
-
         return carry
 
     lax.fori_loop(0, count, coarse_local, 0)
@@ -424,6 +367,7 @@
 
     smoothed_t, through = [], []
     for at in range(count):
+        wait_y(smooth_bufs, smooth_sems, at)
         wait_xz(smooth_bufs, smooth_sems, at)
         blocks = [own_block[at]]
         for side in range(6):
@@ -532,7 +476,7 @@
     count, modes, dofs = near_modes.shape[2:]
     face = face_blocks.shape[4]
     n_z = sizes[2]
-    any_space = pl.BlockSpec(memory_space=pl.ANY)
+    any_space = pl.BlockSpec(memory_space=pltpu.HBM)
     vmem = pl.BlockSpec(memory_space=pltpu.VMEM)
     f32, bf16 = jnp.float32, jnp.bfloat16
     dma = pltpu.SemaphoreType.DMA
@@ -553,7 +497,7 @@
             pltpu.VMEM((count + 2, modes, dofs), f32),
             pltpu.VMEM((count, dofs, dofs), f32),
             pltpu.VMEM((count, 6, face, dofs), f32),
-            pltpu.VMEM((count, 6, face), jnp.int32),
+            pltpu.VMEM((6, count, face), jnp.int32),
             pltpu.VMEM((count, modes, modes), f32),
             pltpu.VMEM((count, dofs, dofs), bf16),
             pltpu.VMEM((count, dofs, dofs), bf16),
@@ -573,9 +517,9 @@
             dma((3,)),
             dma((count,)),
             dma((count,)),
-            dma((7, count)),
             dma((6, count)),
-            dma((7, count)),
+            dma((6, count)),
+            dma((6, count)),
             dma((6, count)),
             dma((6,)),
             dma((6,)),
@@ -585,10 +529,10 @@
             dma((n_z - 1,)),
         ],
         compiler_params=pltpu.CompilerParams(
-            collective_id=0, has_side_effects=True, vmem_limit_bytes=48 * 2**20
+            collective_id=0, has_side_effects=True, vmem_limit_bytes=2**26 - 10550 * 1024
         ),
         cost_estimate=pl.CostEstimate(flops=2 * 10**9, bytes_accessed=11 * 10**6, transcendentals=0),
-    )(near_modes, diag_blocks, face_blocks, face_rows, coarse_modes)
+    )(near_modes, diag_blocks, face_blocks, jnp.transpose(face_rows, (0, 1, 3, 2, 4)), coarse_modes)
     return coarse_one[None, None], column[None, None]
 
 

time: 55.5 us -> 48.3 us (0.87)
  Pallas kernels: 48.8 us -> 44.7 us
  local copies, waits for them, and re-layouts: 5.86 us -> 2.74 us
    pallas_call x1, Pallas kernels: 48.8 us -> 44.7 us  [per_device(): pl.pallas_call(functools.partial(kernel, sizes), out_shape=(jax.ShapeDtyp...]
    unnamed x9 -> x6, local copies, waits for them, and re-layouts: 5.86 us -> 2.74 us
where the time goes in v2:
time: 48.3 us; the launch traced here: 48.1 us
  Pallas kernels  44.7 us (93%)
  local copies, waits for them, and re-layouts  2.74 us (6%)
  between operations  0.65 us (1%)
    pallas_call x1, Pallas kernels, per_device(): pl.pallas_call(functools.partial(kernel, sizes), out_shape=(jax.ShapeDtyp...  44.7 us
    unnamed x6, local copies, waits for them, and re-layouts  2.74 us

profile of v2, /device:TPU:1, one launch (start us, length us, event | category | flops | bytes accessed | tf_op | source)
XLA Modules:
  0.0 48.1 jit_solution(4384259962354058804)
XLA Ops:
  0.6 0.0 copy-start
  0.6 0.8 %copy-done = f32[1,1,4,24,24]{4,3,2,1,0:T(8,128)S(1)} copy-done((f32[1,1,4,24,24]{4,3,2,1,0:T(8,128)S(1)}, f32[1,1,4,24,24]{4,3,2,1,0:T(8,128)}, u32[]{:S(2)}) %copy-start) | copy-done | bytes 9240
  1.4 0.0 copy-start.1
  1.4 0.7 %copy-done.1 = s32[1,1,4,6,128]{4,2,3,1,0:T(4,128)S(1)} copy-done((s32[1,1,4,6,128]{4,2,3,1,0:T(4,128)S(1)}, s32[1,1,4,6,128]{4,2,3,1,0:T(4,128)}, u32[]{:S(2)}) %copy-start.1) | copy-done | bytes 12312
  2.1 44.7 %shard_map.68 = (f32[4,24,168]{2,1,0:T(8,128)S(1)}, f32[24,120]{1,0:T(8,128)S(1)}) custom-call(f32[1,1,4,24,512]{4,3,2,1,0:T(8,128)} %near_hbm.1, f32[1,1,4,512,512]{4,3,2,1,0:T(8,128)} %diag_hbm.1, f32[1,1,4,6,128,512]{5,4,3,2,1,0:T(8,128)} %face_hbm.1, s32[1,1,6,4,128]{4,3,2,1,0:T(4,128)S(1)} %bitcast.4, f32[1,1,4,24,24]{4,3,2,1,0:T(8,128)S(1)} %copy-done), custom_call_target="tpu_custom_call" | custom-call | flops 2000000000 | bytes 11000000 | tf_op jit(solution)/shard_map/pallas_call | solution.py:483
  46.8 0.6 %copy.9 = f32[1,1,4,24,168]{4,3,2,1,0:T(8,128)} copy(f32[1,1,4,24,168]{4,3,2,1,0:T(8,128)S(1)} %bitcast.3) | data formatting | bytes 129024
  47.5 0.6 %copy.10 = f32[1,1,24,120]{3,2,1,0:T(8,128)} copy(f32[1,1,24,120]{3,2,1,0:T(8,128)S(1)} %bitcast.5) | data formatting | bytes 23040
Async XLA Ops:
  0.6 0.8 %copy-start = (f32[1,1,4,24,24]{4,3,2,1,0:T(8,128)S(1)}, f32[1,1,4,24,24]{4,3,2,1,0:T(8,128)}, u32[]{:S(2)}) copy-start(f32[1,1,4,24,24]{4,3,2,1,0:T(8,128)} %modes_hbm.1) | copy-start | bytes 27652
  1.4 0.7 %copy-start.1 = (s32[1,1,4,6,128]{4,2,3,1,0:T(4,128)S(1)}, s32[1,1,4,6,128]{4,2,3,1,0:T(4,128)}, u32[]{:S(2)}) copy-start(s32[1,1,4,6,128]{4,2,3,1,0:T(4,128)} %param.8) | copy-start | bytes 36868

commit v3 on v2

--- a/solution.py
+++ b/solution.py
@@ -8,7 +8,6 @@
 from jax.sharding import PartitionSpec as P
 
 MESH = pl.DeviceIdType.MESH
-HIGHEST = lax.Precision.HIGHEST
 OMEGA_FINE = 2.0 / 3.0
 OMEGA_COARSE = 1.0
 EPSILON = 1e-06
@@ -30,6 +29,15 @@
 def split(value):
     high = value.astype(jnp.bfloat16).astype(jnp.float32)
     return jnp.concatenate([high, value - high], axis=0).astype(jnp.bfloat16)
+
+
+def two_pieces(value):
+    high = value.astype(jnp.bfloat16)
+    return high, (value - high.astype(jnp.float32)).astype(jnp.bfloat16)
+
+
+def product_of(dot, left, right):
+    return fold(dot(left, right[0]) + dot(left, right[1]))
 
 
 def fold(value):
@@ -163,22 +171,6 @@
         def _(side=side):
             modes_halo[side] = jnp.zeros_like(modes_halo[side])
 
-    loads[2].wait()
-    pieces = [modes_in[at].T for at in range(count)]
-    pieces.append(jnp.zeros((modes, LANES - count * modes), jnp.float32))
-    modes_pack[...] = jnp.concatenate(pieces, axis=1)
-    loads[1].wait()
-
-    def build_selector(at, carry):
-        for side in range(6):
-            chosen = rows_in[side, pl.ds(at, 1), :]
-            for start in range(0, dofs, LANES):
-                row = lax.broadcasted_iota(jnp.int32, (LANES, face), 0) + start
-                hit = jnp.where(row == chosen, 1.0, 0.0).astype(jnp.bfloat16)
-                selector[at, pl.ds(start, LANES), pl.ds(side * face, face)] = hit
-        return carry
-
-    lax.fori_loop(0, count, build_selector, 0)
     loads[0].wait()
 
     met = n_z - 1
@@ -205,19 +197,21 @@
         )
 
     def send_halo(bufs, sems, at):
-        for side in (2, 3, 0, 1):
+        for side in (0, 1, 2, 3):
 
             @pl.when(has[side])
             def _(side=side):
                 halo(bufs, sems, side, at, side ^ 1).start()
 
-        @pl.when(has[4] & (at == 0))
-        def _():
-            halo(bufs, sems, 4, at, 5).start()
-
-        @pl.when(has[5] & (at == last))
-        def _():
-            halo(bufs, sems, 5, at, 4).start()
+    def send_z_low(bufs, sems):
+        @pl.when(has[4])
+        def _():
+            halo(bufs, sems, 4, 0, 5).start()
+
+    def send_z_high(bufs, sems):
+        @pl.when(has[5])
+        def _():
+            halo(bufs, sems, 5, last, 4).start()
 
     def wait_y(bufs, sems, at):
         for side in (2, 3):
@@ -242,19 +236,21 @@
             halo(bufs, sems, 5, 0, 5).wait_recv()
 
     def wait_sent(bufs, sems, at):
-        for side in (2, 3, 0, 1):
+        for side in (0, 1, 2, 3):
 
             @pl.when(has[side])
             def _(side=side):
                 halo(bufs, sems, side, at, side ^ 1).wait_send()
 
-        @pl.when(has[4] & (at == 0))
-        def _():
-            halo(bufs, sems, 4, at, 5).wait_send()
-
-        @pl.when(has[5] & (at == last))
-        def _():
-            halo(bufs, sems, 5, at, 4).wait_send()
+
+    def wait_sent_z(bufs, sems):
+        @pl.when(has[4])
+        def _():
+            halo(bufs, sems, 4, 0, 5).wait_send()
+
+        @pl.when(has[5])
+        def _():
+            halo(bufs, sems, 5, last, 4).wait_send()
 
     near_bufs, near_sems = (near_x, near_y, near_z), (near_send, near_recv)
     smooth_bufs, smooth_sems = (smooth_x, smooth_y, smooth_z), (smooth_send, smooth_recv)
@@ -264,7 +260,13 @@
         return carry
 
     lax.fori_loop(0, count, send_near, 0)
-
+    send_z_low(near_bufs, near_sems)
+    send_z_high(near_bufs, near_sems)
+
+    loads[2].wait()
+    pieces = [modes_in[at].T for at in range(count)]
+    pieces.append(jnp.zeros((modes, LANES - count * modes), jnp.float32))
+    modes_pack[...] = jnp.concatenate(pieces, axis=1)
     def modes_copy(side, landing):
         return pltpu.make_async_remote_copy(
             src_ref=modes_pack,
@@ -281,6 +283,18 @@
         def _(side=side):
             modes_copy(side, side ^ 1).start()
 
+    loads[1].wait()
+
+    def build_selector(at, carry):
+        for side in range(6):
+            chosen = rows_in[side, pl.ds(at, 1), :]
+            for start in range(0, dofs, LANES):
+                row = lax.broadcasted_iota(jnp.int32, (LANES, face), 0) + start
+                hit = jnp.where(row == chosen, 1.0, 0.0).astype(jnp.bfloat16)
+                selector[at, pl.ds(start, LANES), pl.ds(side * face, face)] = hit
+        return carry
+
+    lax.fori_loop(0, count, build_selector, 0)
     def own_product(at, carry):
         load_diag(at).wait()
         split_into(diag_in.at[at], diag_high.at[at], diag_low.at[at], dofs, 64)
@@ -297,12 +311,17 @@
 
     lax.fori_loop(0, count, own_product, 0)
 
-    def smooth(at, carry):
+    def split_faces(at, carry):
         load_face(at).wait()
         for side in range(6):
             split_into(
                 face_in.at[at, side], face_high.at[at, side], face_low.at[at, side], face, 64
             )
+        return carry
+
+    lax.fori_loop(0, count, split_faces, 0)
+
+    def smooth(at, carry):
         wait_y(near_bufs, near_sems, at)
         wait_xz(near_bufs, near_sems, at)
 
@@ -322,6 +341,14 @@
         total = product[at] + fold(dot_nt(terms, selector[at]))
         smooth_z[at + 1] = near_z[at + 1] - OMEGA_FINE * total / diagonal[at]
         send_halo(smooth_bufs, smooth_sems, at)
+
+        @pl.when(at == 0)
+        def _():
+            send_z_low(smooth_bufs, smooth_sems)
+
+        @pl.when(at == last)
+        def _():
+            send_z_high(smooth_bufs, smooth_sems)
         return carry
 
     lax.fori_loop(0, count, smooth, 0)
@@ -362,7 +389,9 @@
     for at in range(count):
         sides = [lane_block(modes_halo[side], at) for side in range(4)]
         around.append(
-            jnp.concatenate([along_z[at + 1]] + sides + [along_z[at], along_z[at + 2]], axis=1)
+            split(
+                jnp.concatenate([along_z[at + 1]] + sides + [along_z[at], along_z[at + 2]], axis=1)
+            )
         )
 
     smoothed_t, through = [], []
@@ -377,15 +406,17 @@
                 value = smooth_y[side - 2, at]
             else:
                 value = smooth_z[at + 2 * (side - 4)]
-            lateral = fold(dot_nt(reach[at, side], split(value)))
-            blocks.append(lateral[:, :modes] + lateral[:, modes:])
+            blocks.append(product_of(dot_nt, reach[at, side], two_pieces(value)))
         coarse = jnp.concatenate(blocks, axis=1)
         coarse_out[at] = coarse
-        scale = dot_nt(jnp.ones_like(coarse), jnp.abs(coarse), HIGHEST) + EPSILON
-        applied = dot_nt(around[at], coarse, HIGHEST)
+        sizes_high, sizes_low = two_pieces(jnp.abs(coarse))
+        ones = jnp.ones(coarse.shape, jnp.bfloat16)
+        scale = dot_nt(ones, sizes_high) + dot_nt(ones, sizes_low) + EPSILON
+        coarse = two_pieces(coarse)
+        applied = product_of(dot_nt, around[at], coarse)
         result = along_z[at + 1] - OMEGA_COARSE * applied / scale
         smoothed_t.append(result)
-        through.append(dot_nn(result, coarse, HIGHEST))
+        through.append(product_of(dot_nn, split(result), coarse))
 
     right_rows = [1, 2, 3, 4, 0, 0]
     filler = jnp.zeros((modes, LANES - count * modes), jnp.float32)
@@ -435,7 +466,7 @@
         def _(side=side):
             result_copy(side, side).wait_recv()
 
-    part[...] = dot_nt(left[...], right[...], HIGHEST)
+    part[...] = product_of(dot_nt, split(left[...]), two_pieces(right[...]))
     gathered[gz] = part[...]
     shares = [
         pltpu.make_async_remote_copy(
@@ -457,6 +488,8 @@
         return carry
 
     lax.fori_loop(0, count, finish, 0)
+    wait_sent_z(near_bufs, near_sems)
+    wait_sent_z(smooth_bufs, smooth_sems)
     for side in range(6):
 
         @pl.when(has[side])

time: 48.3 us -> 46.9 us (0.971)
  Pallas kernels: 44.7 us -> 43.3 us
    pallas_call x1, Pallas kernels: 44.7 us -> 43.3 us  [per_device(): pl.pallas_call(functools.partial(kernel, sizes), out_shape=(jax.ShapeDtyp...]
where the time goes in v3:
time: 46.9 us; the launch traced here: 46.7 us
  Pallas kernels  43.3 us (92%)
  local copies, waits for them, and re-layouts  2.74 us (6%)
  between operations  0.65 us (1%)
    pallas_call x1, Pallas kernels, per_device(): pl.pallas_call(functools.partial(kernel, sizes), out_shape=(jax.ShapeDtyp...  43.3 us
    unnamed x6, local copies, waits for them, and re-layouts  2.74 us

profile of v3, /device:TPU:1, one launch (start us, length us, event | category | flops | bytes accessed | tf_op | source)
XLA Modules:
  0.0 46.7 jit_solution(17394568423752649149)
XLA Ops:
  0.6 0.0 copy-start
  0.6 0.8 %copy-done = f32[1,1,4,24,24]{4,3,2,1,0:T(8,128)S(1)} copy-done((f32[1,1,4,24,24]{4,3,2,1,0:T(8,128)S(1)}, f32[1,1,4,24,24]{4,3,2,1,0:T(8,128)}, u32[]{:S(2)}) %copy-start) | copy-done | bytes 9240
  1.4 0.0 copy-start.1
  1.4 0.7 %copy-done.1 = s32[1,1,4,6,128]{4,2,3,1,0:T(4,128)S(1)} copy-done((s32[1,1,4,6,128]{4,2,3,1,0:T(4,128)S(1)}, s32[1,1,4,6,128]{4,2,3,1,0:T(4,128)}, u32[]{:S(2)}) %copy-start.1) | copy-done | bytes 12312
  2.1 43.3 %shard_map.68 = (f32[4,24,168]{2,1,0:T(8,128)S(1)}, f32[24,120]{1,0:T(8,128)S(1)}) custom-call(f32[1,1,4,24,512]{4,3,2,1,0:T(8,128)} %near_hbm.1, f32[1,1,4,512,512]{4,3,2,1,0:T(8,128)} %diag_hbm.1, f32[1,1,4,6,128,512]{5,4,3,2,1,0:T(8,128)} %face_hbm.1, s32[1,1,6,4,128]{4,3,2,1,0:T(4,128)S(1)} %bitcast.4, f32[1,1,4,24,24]{4,3,2,1,0:T(8,128)S(1)} %copy-done), custom_call_target="tpu_custom_call" | custom-call | flops 2000000000 | bytes 11000000 | tf_op jit(solution)/shard_map/pallas_call | solution.py:516
  45.5 0.6 %copy.9 = f32[1,1,4,24,168]{4,3,2,1,0:T(8,128)} copy(f32[1,1,4,24,168]{4,3,2,1,0:T(8,128)S(1)} %bitcast.3) | data formatting | bytes 129024
  46.1 0.6 %copy.10 = f32[1,1,24,120]{3,2,1,0:T(8,128)} copy(f32[1,1,24,120]{3,2,1,0:T(8,128)S(1)} %bitcast.5) | data formatting | bytes 23040
Async XLA Ops:
  0.6 0.8 %copy-start = (f32[1,1,4,24,24]{4,3,2,1,0:T(8,128)S(1)}, f32[1,1,4,24,24]{4,3,2,1,0:T(8,128)}, u32[]{:S(2)}) copy-start(f32[1,1,4,24,24]{4,3,2,1,0:T(8,128)} %modes_hbm.1) | copy-start | bytes 27652
  1.4 0.7 %copy-start.1 = (s32[1,1,4,6,128]{4,2,3,1,0:T(4,128)S(1)}, s32[1,1,4,6,128]{4,2,3,1,0:T(4,128)}, u32[]{:S(2)}) copy-start(s32[1,1,4,6,128]{4,2,3,1,0:T(4,128)} %param.8) | copy-start | bytes 36868

commit v4 on v3

--- a/solution.py
+++ b/solution.py
@@ -12,6 +12,7 @@
 OMEGA_COARSE = 1.0
 EPSILON = 1e-06
 LANES = 128
+WIDTH = 4
 
 
 def dot_nt(left, right, precision=None):
@@ -115,7 +116,14 @@
         {"gz": gz - 1},
         {"gz": gz + 1},
     ]
-    peers = [lax.rem(gz + step, n_z) for step in range(1, n_z)]
+    width = WIDTH if n_z % WIDTH == 0 else 1
+    height = n_z // width
+    steps = [(step_y, step_x) for step_y in range(height) for step_x in range(width)][1:]
+    steps.sort(key=lambda step: -min(step[0], height - step[0]) - min(step[1], width - step[1]))
+    peers = [
+        lax.rem(gz // width + step_y, height) * width + lax.rem(lax.rem(gz, width) + step_x, width)
+        for step_y, step_x in steps
+    ]
 
     loads = [
         pltpu.make_async_copy(near_hbm.at[0, 0], near_z.at[pl.ds(1, count)], load_sem.at[0]),
@@ -139,14 +147,14 @@
     right[...] = jnp.zeros_like(right)
 
     barrier = pltpu.get_barrier_semaphore()
-    for side in range(4):
-
-        @pl.when(has[side])
-        def _(side=side):
-            pl.semaphore_signal(barrier, inc=1, device_id=target[side], device_id_type=MESH)
-
     for peer in peers:
         pl.semaphore_signal(barrier, inc=1, device_id={"gz": peer}, device_id_type=MESH)
+
+    for side in range(4):
+
+        @pl.when(has[side])
+        def _(side=side):
+            pl.semaphore_signal(barrier, inc=1, device_id=target[side], device_id_type=MESH)
 
     for side in range(2):
 

time: 46.9 us -> 46.7 us (level)
  no operation moved by 1% of the time
where the time goes in v4:
time: 46.7 us; the launch traced here: 46.5 us
  Pallas kernels  43.1 us (92%)
  local copies, waits for them, and re-layouts  2.74 us (6%)
  between operations  0.65 us (1%)
    pallas_call x1, Pallas kernels, per_device(): pl.pallas_call(functools.partial(kernel, sizes), out_shape=(jax.ShapeDtyp...  43.1 us
    unnamed x6, local copies, waits for them, and re-layouts  2.74 us

profile of v4, /device:TPU:1, one launch (start us, length us, event | category | flops | bytes accessed | tf_op | source)
XLA Modules:
  0.0 46.5 jit_solution(10899095013076375717)
XLA Ops:
  0.6 0.0 copy-start
  0.6 0.8 %copy-done = f32[1,1,4,24,24]{4,3,2,1,0:T(8,128)S(1)} copy-done((f32[1,1,4,24,24]{4,3,2,1,0:T(8,128)S(1)}, f32[1,1,4,24,24]{4,3,2,1,0:T(8,128)}, u32[]{:S(2)}) %copy-start) | copy-done | bytes 9240
  1.4 0.0 copy-start.1
  1.4 0.7 %copy-done.1 = s32[1,1,4,6,128]{4,2,3,1,0:T(4,128)S(1)} copy-done((s32[1,1,4,6,128]{4,2,3,1,0:T(4,128)S(1)}, s32[1,1,4,6,128]{4,2,3,1,0:T(4,128)}, u32[]{:S(2)}) %copy-start.1) | copy-done | bytes 12312
  2.1 43.1 %shard_map.68 = (f32[4,24,168]{2,1,0:T(8,128)S(1)}, f32[24,120]{1,0:T(8,128)S(1)}) custom-call(f32[1,1,4,24,512]{4,3,2,1,0:T(8,128)} %near_hbm.1, f32[1,1,4,512,512]{4,3,2,1,0:T(8,128)} %diag_hbm.1, f32[1,1,4,6,128,512]{5,4,3,2,1,0:T(8,128)} %face_hbm.1, s32[1,1,6,4,128]{4,3,2,1,0:T(4,128)S(1)} %bitcast.4, f32[1,1,4,24,24]{4,3,2,1,0:T(8,128)S(1)} %copy-done), custom_call_target="tpu_custom_call" | custom-call | flops 2000000000 | bytes 11000000 | tf_op jit(solution)/shard_map/pallas_call | solution.py:524
  45.3 0.6 %copy.9 = f32[1,1,4,24,168]{4,3,2,1,0:T(8,128)} copy(f32[1,1,4,24,168]{4,3,2,1,0:T(8,128)S(1)} %bitcast.3) | data formatting | bytes 129024
  45.9 0.6 %copy.10 = f32[1,1,24,120]{3,2,1,0:T(8,128)} copy(f32[1,1,24,120]{3,2,1,0:T(8,128)S(1)} %bitcast.5) | data formatting | bytes 23040
Async XLA Ops:
  0.6 0.8 %copy-start = (f32[1,1,4,24,24]{4,3,2,1,0:T(8,128)S(1)}, f32[1,1,4,24,24]{4,3,2,1,0:T(8,128)}, u32[]{:S(2)}) copy-start(f32[1,1,4,24,24]{4,3,2,1,0:T(8,128)} %modes_hbm.1) | copy-start | bytes 27652
  1.4 0.7 %copy-start.1 = (s32[1,1,4,6,128]{4,2,3,1,0:T(4,128)S(1)}, s32[1,1,4,6,128]{4,2,3,1,0:T(4,128)}, u32[]{:S(2)}) copy-start(s32[1,1,4,6,128]{4,2,3,1,0:T(4,128)} %param.8) | copy-start | bytes 36868
